TPU v7x, 32 devices: a whole 2x2x4 slice. The times are simulated.
32 devices in a mesh: dp: 8 (over y, x, core), shard: 4 (over z).
Axes of the slice: x: 2, y: 2, z: 4, core: 2. Of those that a mesh axis runs over, the one named last changes fastest.
Arguments:
- features: bfloat16 [65536, 2048], P(('dp', 'shard')), may hold values from -6 to 6
- neighbors: int32 [65536, 128], P(('dp', 'shard')), may hold values from -1 to 1023, as said below
- weight: bfloat16 [2048, 2048], P(('dp', 'shard')), may hold values from -0.125 to 0.125
- bias_terms: bfloat16 [2048], P(('dp', 'shard')), may hold values from -1.796875 to 1.796875
- grad_out: bfloat16 [65536, 2048], P(('dp', 'shard')), may hold values from -6 to 6
Outputs:
- activations: bfloat16 [65536, 2048], P(('dp', 'shard'))
- grad_features: float32 [65536, 2048], P(('dp', 'shard'))
- grad_weight: float32 [2048, 2048], P(('dp', 'shard'))
- grad_bias: float32 [2048], P(('dp', 'shard'))
Inputs may be any that keep to these rules, and one draw needn't show every extreme that they name: `neighbors`: each row lists neighbours of its node as indices within its cluster (clusters are aligned blocks of 1024 rows): used slots first, then -1 pads. An index may repeat; each slot counts as one edge. Every row has at least one neighbour, and the first row of every cluster uses all 128 slots.
All inputs are finite; a program needn't handle non-finite values.
Results may differ from a plain program's by a relative error of at most 0.0057.
Values may be sent and summed in bfloat16 or wider, within the bound.
A program may use at most 192 MiB of HBM per device.

v0:
```python
import jax
import jax.numpy as jnp
from jax import lax
from jax.sharding import PartitionSpec as P

CLUSTER = 1024
SLOTS = 128


def adjacency(neighbor_blocks):
    cluster_count, node_total, slot_total = neighbor_blocks.shape
    cluster_ids = lax.broadcasted_iota(jnp.int32, neighbor_blocks.shape, 0)
    row_ids = lax.broadcasted_iota(jnp.int32, neighbor_blocks.shape, 1)
    targets = jnp.where(neighbor_blocks >= 0, neighbor_blocks, node_total)
    counted = jnp.zeros((cluster_count, node_total, node_total), jnp.float32)
    counted = counted.at[cluster_ids, row_ids, targets].add(1.0, mode="drop")
    return counted.astype(jnp.bfloat16)


def smooth_gate(values):
    return jax.nn.gelu(values, approximate=True)


def on_device(features, neighbors, weight, bias_terms, grad_out):
    node_count, feature_width = features.shape
    cluster_count = node_count // CLUSTER
    full_weight, full_bias = (
        lax.all_gather(weight, ("dp", "shard"), axis=0, tiled=True),
        lax.all_gather(bias_terms, ("dp", "shard"), axis=0, tiled=True),
    )
    linkage = adjacency(neighbors.reshape(cluster_count, CLUSTER, SLOTS))
    degree = jnp.sum((neighbors >= 0).astype(jnp.float32), axis=1, keepdims=True)
    factor = 1.0 / (degree + 1.0)
    blocks = features.reshape(cluster_count, CLUSTER, feature_width)
    summed = jnp.einsum(
        "cij,cjf->cif", linkage, blocks, preferred_element_type=jnp.float32
    ).reshape(node_count, feature_width)
    mixed_rows = (factor * (2.0 * features.astype(jnp.float32) + summed)).astype(jnp.bfloat16)
    linear = jnp.dot(
        mixed_rows, full_weight, preferred_element_type=jnp.float32
    ) + full_bias.astype(jnp.float32)
    gated, gate_pull = jax.vjp(smooth_gate, linear)
    output = gated.astype(jnp.bfloat16)
    grad_linear = gate_pull(grad_out.astype(jnp.float32))[0].astype(jnp.bfloat16)
    local_weight = lax.dot_general(
        mixed_rows, grad_linear, (((0,), (0,)), ((), ())), preferred_element_type=jnp.float32
    )
    local_bias = jnp.sum(grad_linear.astype(jnp.float32), axis=0)
    grad_weight, grad_bias = (
        lax.psum_scatter(local_weight, ("dp", "shard"), scatter_dimension=0, tiled=True),
        lax.psum_scatter(local_bias, ("dp", "shard"), scatter_dimension=0, tiled=True),
    )
    back_weight = lax.all_gather(weight, ("dp", "shard"), axis=0, tiled=True)
    grad_mixed = lax.dot_general(
        grad_linear, back_weight, (((1,), (1,)), ((), ())), preferred_element_type=jnp.float32
    )
    spread = (factor * grad_mixed).astype(jnp.bfloat16)
    returned = jnp.einsum(
        "cji,cjf->cif",
        linkage,
        spread.reshape(cluster_count, CLUSTER, feature_width),
        preferred_element_type=jnp.float32,
    )
    grad_features = 2.0 * spread.astype(jnp.float32) + returned.reshape(node_count, feature_width)
    return (output, grad_features, grad_weight, grad_bias)


def solution(mesh):
    return jax.shard_map(
        on_device,
        mesh=mesh,
        in_specs=(
            P(("dp", "shard"), None),
            P(("dp", "shard"), None),
            P(("dp", "shard"), None),
            P(("dp", "shard")),
            P(("dp", "shard"), None),
        ),
        out_specs=(
            P(("dp", "shard"), None),
            P(("dp", "shard"), None),
            P(("dp", "shard"), None),
            P(("dp", "shard")),
        ),
        check_vma=False,
    )
```

profile of v0, /device:TPU:0, one launch (start us, length us, event | category | flops | bytes accessed | tf_op | source)
XLA Modules:
  0.0 1927.7 jit_solution(4052041602231505846)
XLA Ops:
  7.2 0.0 copy-start.3
  7.2 0.0 all-gather.2.cloned.1.call-start
  7.2 0.7 all-gather.2.cloned.1.call-update
  7.9 0.0 reduce-scatter.2.cloned.1.call-start
  8.0 0.9 dynamic-update-slice
  8.8 42.8 %all-reduce = bf16[2048]{0:T(1024)(128)(2,1)S(1)} all-reduce(bf16[2048]{0:T(1024)(128)(2,1)S(1)} %dynamic-update-slice), channel_id=1, replica_groups=mesh['dp'=8,'shard'=4] {'dp','shard'}, use_global_device_ids=true, to_apply=%add | all-reduce | flops 2048 | bytes 8192
  51.7 1.4 compare_select_fusion
  53.1 0.1 iota.13
  53.1 0.1 iota.12
  53.2 1.1 multiply_reduce_fusion
  54.3 0.0 copy-done.3
  54.3 0.6 and_reduce_fusion
  54.9 0.1 broadcast_select_fusion
  55.0 0.1 broadcast.106
  55.1 1409.0 %scatter_custom_fusion = f32[2097152]{0:T(1024)} fusion(s32[262144]{0:T(1024)S(1)} %bitcast.25, f32[262144]{0:T(1024)S(1)} %broadcast.106, f32[]{:T(128)} %constant.12.clone.1), kind=kCustom, calls=%fused_computation.22 | custom fusion | flops 262144 | bytes 8388612
  1464.1 5.2 convert_element_type.44
  1469.3 7.3 reshape.67
  1476.5 0.0 copy-done.2
  1476.5 0.2 convert_reduce_fusion.1
  1476.8 11.9 fusion.15
  1488.6 8.5 fusion.11
  1497.2 38.1 %convert_reduce_fusion = (f32[2048]{0:T(1024)S(1)}, bf16[2048,2048]{1,0:T(8,128)(2,1)}, bf16[2048,2048]{1,0:T(8,128)(2,1)}) fusion(f32[2048]{0:T(1024)S(1)} %convert_element_type.37, bf16[2048,2048]{1,0:T(8,128)(2,1)} %param.9, bf16[2048,2048]{1,0:T(8,128)(2,1)} %fusion.11, bf16[2048,2048]{1,0:T(8,128)(2,1)} %all-gather.2.cloned.1.call-done), kind=kOutput, calls=%fused_computation.19 | convolution fusion | flops 17288919040 | bytes 41959424 | tf_op jit(solution)/shard_map/dot_general | solution.py:39
  1535.2 0.0 copy-done
  1535.2 22.8 %fusion.17 = f32[2048,2048]{1,0:T(8,128)} fusion(bf16[2048,2048]{1,0:T(8,128)(2,1)S(1)} %copy-done, bf16[2048,2048]{1,0:T(8,128)(2,1)} %get-tuple-element.5), kind=kOutput, calls=%fused_computation.34 | convolution fusion | flops 17179869184 | bytes 33554432 | tf_op jit(solution)/shard_map/dot_general | solution.py:45
  1558.1 0.0 reduce-scatter.2.cloned.1.call-update
  1558.1 42.1 %all-reduce.1 = f32[2048]{0:T(1024)S(1)} all-reduce(f32[2048]{0:T(1024)S(1)} %get-tuple-element.4), channel_id=3, replica_groups=mesh['dp'=8,'shard'=4] {'dp','shard'}, use_global_device_ids=true, to_apply=%region_4.5.clone | all-reduce | flops 2048 | bytes 16384
  1600.2 0.6 dynamic-slice
  1600.8 23.9 %multiply_convert_fusion = bf16[2048,2048]{1,0:T(8,128)(2,1)} fusion(bf16[2048,2048]{1,0:T(8,128)(2,1)} %get-tuple-element.5, bf16[2048,2048]{1,0:T(8,128)(2,1)} %all-gather.2.cloned.1.call-done, f32[2048]{0:T(1024)S(1)} %add_divide_fusion), kind=kOutput, calls=%fused_computation.20 | convolution fusion | flops 17188257792 | bytes 25174016 | tf_op jit(solution)/shard_map/dot_general | solution.py:54
  1624.8 0.0 copy-done.1
  1624.8 12.0 fusion.16
  1636.8 11.0 bitcast_add_fusion
  1647.9 273.0 %reduce-scatter.2.cloned.1.call-done = f32[64,2048]{1,0:T(8,128)} async-done(((f32[2048,2048]{1,0:T(8,128)}), f32[64,2048]{1,0:T(8,128)}) %reduce-scatter.2.cloned.1.call-update) | async-done | bytes 524304 | tf_op jit(solution)/shard_map/reduce_scatter | solution.py:50
  (7 shorter events, 0.0 us)
Async XLA Ops:
  7.2 47.2 %copy-start.3 = (s32[3]{0:T(128)S(1)}, s32[3]{0:T(128)}, u32[]{:S(2)}) copy-start(s32[3]{0:T(128)} %constant.33) | copy-start | bytes 40
  7.2 1490.0 %all-gather.2.cloned.1.call-start = ((), (), s32[]{:S(2)}) async-start(), calls=%async_computation.1 | async-start | bytes 8650752 | tf_op jit(solution)/shard_map/all_gather | solution.py:28
  7.9 1913.0 %reduce-scatter.2.cloned.1.call-start = ((), (), s32[]{:S(2)}) async-start(), calls=%async_computation.2 | async-start | bytes 17301504 | tf_op jit(solution)/shard_map/reduce_scatter | solution.py:50
  1464.1 12.4 copy-start.2
  1497.2 38.1 %copy-start = (bf16[2048,2048]{1,0:T(8,128)(2,1)S(1)}, bf16[2048,2048]{1,0:T(8,128)(2,1)}, u32[]{:S(2)}) copy-start(bf16[2048,2048]{1,0:T(8,128)(2,1)} %fusion.11) | copy-start | bytes 25165828
  1600.8 23.9 %copy-start.1 = (bf16[2,1024,1024]{2,1,0:T(8,128)(2,1)S(1)}, bf16[2,1024,1024]{2,1,0:T(8,128)(2,1)}, u32[]{:S(2)}) copy-start(bf16[2,1024,1024]{2,1,0:T(8,128)(2,1)} %reshape.67) | copy-start | bytes 12582916
Sparse Core Ops, SparseCore 0:
  10.9 81.1 all-gather.1
  1558.2 362.6 reduce-scatter.1
where the time goes:
time: 1930 us
  other arithmetic  1440 us (75%)
  waiting for transfers between devices  274 us (14%)
  matrix products  109 us (6%)
  blocking collectives  85 us (4%)
    unnamed x4, other arithmetic  1410 us
    reduce_scatter x1, waiting for transfers between devices, on_device(): lax.psum_scatter(local_weight, ('dp', 'shard'), scatter_dimension=0, tile...  273 us
    unnamed x2, blocking collectives  85 us
  transfers between devices with their start and end apart: 2, of which 1 were waited for; matrix products, arithmetic and copies ran while one was open for 77% of the time, Pallas kernels for 0%

commit v1 on v0

v1 whole, which is shorter than its diff:
```python
import jax
import jax.numpy as jnp
from jax import lax
from jax.experimental import pallas as pl
from jax.experimental.pallas import tpu as pltpu
from jax.sharding import PartitionSpec as P

F32, BF16, I32 = jnp.float32, jnp.bfloat16, jnp.int32
MESH = pl.DeviceIdType.MESH
CLUSTER = 1024
SLOTS = 128
UNROLL = 16
PC = 512
HC = 256
ALPHA = 0.7978845608028654
BETA = ALPHA * 0.044715
NN = (((1,), (0,)), ((), ()))
TN = (((0,), (0,)), ((), ()))
NT = (((1,), (1,)), ((), ()))
ALL = slice(None)

GATHER = ("zxy", "zyx", "zxy", "zyx", "xzy", "yzx", "zxy", "zyx")
SCATTER = ("yxz", "xyz", "yzx", "xzy", "yxz", "xyz", "yxz", "xyz")
COUNT_EVENTS = (
    (3, "second", 0),
    (3, "first", 1),
    (5, "third", 0),
    (6, "second", 1),
    (6, "second", 2),
    (8, "third", 1),
    (8, "first", 3),
    (9, "pass", 0),
    (12, "third", 2),
    (12, "second", 3),
    (13, "pass", 1),
    (15, "third", 3),
)
MIX_EVENTS = ((4, "pass", 2),)
SUM_EVENTS = ((4, 1, 0), (6, 1, 1), (7, 2, 0))
BACK_EVENTS = (
    (0, 3, 0),
    (1, 2, 1),
    (2, 1, 2),
    (3, 3, 1),
    (4, 2, 2),
    (5, 1, 3),
    (6, 3, 2),
    (7, 2, 3),
)


def dot(a, b, dims):
    return lax.dot_general(a, b, dims, preferred_element_type=F32)


class Place:
    def __init__(self, dp_size, shard_size):
        dp, self.z = lax.axis_index("dp"), lax.axis_index("shard")
        self.dp = dp
        self.c, self.x, self.y = dp % 2, (dp // 2) % 2, dp // 4
        self.size = {"c": 2, "x": 2, "y": dp_size // 4, "z": shard_size}

    def at(self, dim):
        return {"c": self.c, "x": self.x, "y": self.y, "z": self.z}[dim]

    def shifted(self, dim, offset):
        size = self.size[dim]
        return lax.rem(self.at(dim) + (offset + size), size)

    def peer(self, dim, offset):
        other = self.shifted(dim, offset)
        if dim == "z":
            return (self.dp, other)
        step = {"c": 1, "x": 2, "y": 4}[dim]
        return (self.dp + step * (other - self.at(dim)), self.z)

    def offsets(self, dim):
        return range(1, self.size[dim])


class Sems:
    def __init__(self):
        self.index = {}

    def __getitem__(self, name):
        return self.index.setdefault(name, len(self.index))


def sem_names(sizes):
    sems = Sems()
    for t in list(range(len(GATHER))) + ["bias"]:
        path = GATHER[0] if t == "bias" else GATHER[t]
        for k in range(3):
            for o in range(1, sizes[path[k]]):
                sems["gather", t, k, o]
        sems["core", t, 0]
        for o in range(1, sizes[path[2]]):
            sems["core", t, o]
    for t in list(range(len(SCATTER))) + ["bias"]:
        path = SCATTER[0] if t == "bias" else SCATTER[t]
        for k in range(3):
            for o in range(1, sizes[path[k]]):
                for h in range(2 if k == 0 and path[0] == "x" else 1):
                    sems["scatter", t, k, o, h]
    sems["swap", "bias"]
    for s in range(len(SCATTER)):
        sems["swap", s]
    return sems


def linkable(rows):
    return rows % 16 == 0


def make_kernel(dp_size, shard_size, rows, width, nodes):
    sizes = {"c": 2, "x": 2, "y": dp_size // 4, "z": shard_size}
    Y, X, S, R = sizes["y"], 2, shard_size, rows
    SR = S * R
    n_dev = dp_size * shard_size
    panels = width // PC
    half_rows = width // 2
    clusters = nodes // CLUSTER
    sems = sem_names(sizes)
    n_sems = len(sems.index)
    chunks = nodes // 128
    TM = 512
    tiles = (nodes // TM) * panels
    per_panel = nodes // TM
    FW = width // Y

    def stage_shape(path, k):
        n = sizes[path[k]] - 1
        left = path[k + 1 :]
        lead = tuple(sizes[d] for d in "yx" if d in left)
        return (n,) + lead, ("z" in left)

    def stage_shapes():
        out = []
        for t in range(len(SCATTER)):
            for k in range(3):
                lead, z = stage_shape(SCATTER[t], k)
                out.append(pltpu.VMEM(lead + (SR if z else R, HC), BF16))
        for k in range(3):
            lead, z = stage_shape(SCATTER[0], k)
            out.append(pltpu.VMEM(lead + (S if z else 1, 8, 128), F32))
        return out

    n_stage = 3 * (len(SCATTER) + 1)
    linked = linkable(rows)

    def kernel(
        f_hbm, n_hbm, w_hbm, b_hbm, g_hbm,
        act_hbm, sp_hbm, a_hbm, gw_hbm, gb_hbm,
        fg, mixed, wg, a2t, fac, bt, brow, gbacc, cr, crb, ptb, gws, gbs, *rest,
    ):
        stage = rest[:n_stage]
        ssem, rsem, lsem = rest[n_stage:]
        me = Place(dp_size, shard_size)
        c, x, y, z = me.c, me.x, me.y, me.z
        started = []

        def remote(name, src, dst, device):
            i = sems[name]
            return pltpu.make_async_remote_copy(
                src_ref=src, dst_ref=dst, send_sem=ssem.at[i], recv_sem=rsem.at[i],
                device_id=device, device_id_type=MESH,
            )

        def send(name, make):
            remote(name, *make()).start()
            started.append((name, make))

        def arrived(name, ref):
            remote(name, ref, ref, me.peer("c", 1)).wait_recv()

        def view(t, core, **at):
            ys, xs = at.get("y", ALL), at.get("x", ALL)
            if t == "bias":
                zs = pl.ds(at["z"], 1) if "z" in at else ALL
                return bt.at[ys, xs, core, zs]
            zs = pl.ds(pl.multiple_of(at["z"] * R, R), R) if "z" in at else ALL
            return wg.at[t // 2, ys, xs, core, zs, pl.ds(t % 2 * HC, HC)]

        own = {"x": x, "y": y, "z": z}

        def fixed(dims):
            return {d: own[d] for d in dims}

        def gather_path(t):
            return GATHER[0] if t == "bias" else GATHER[t]

        def gather_first(t):
            path = gather_path(t)

            def make(o):
                if t == "bias":
                    return b_hbm, bt.at[y, x, c, z], me.peer(path[0], o)
                src = w_hbm.at[:, pl.ds(t * HC, HC)]
                return src, view(t, c, **fixed("xyz")), me.peer(path[0], o)

            for o in me.offsets(path[0]):
                send(("gather", t, 0, o), lambda o=o: make(o))

        def gather_wait(t, k):
            path = gather_path(t)
            for o in me.offsets(path[k]):
                at = fixed(path[k:])
                at[path[k]] = me.shifted(path[k], -o)
                arrived(("gather", t, k, o), view(t, c, **at))

        def gather_send(t, k):
            path = gather_path(t)

            def make(o):
                ref = view(t, c, **fixed(path[k:]))
                return ref, ref, me.peer(path[k], o)

            for o in me.offsets(path[k]):
                send(("gather", t, k, o), lambda o=o: make(o))

        def core_send(t, late):
            path = gather_path(t)

            def make(o):
                at = {path[2]: me.shifted(path[2], -o)} if o else fixed(path[2:])
                ref = view(t, c, **at)
                return ref, ref, me.peer("c", 1)

            for o in me.offsets(path[2]) if late else (0,):
                send(("core", t, o), lambda o=o: make(o))

        def core_wait(t):
            path = gather_path(t)
            arrived(("core", t, 0), view(t, 1 - c, **fixed(path[2:])))
            for o in me.offsets(path[2]):
                arrived(
                    ("core", t, o),
                    view(t, 1 - c, **{path[2]: me.shifted(path[2], -o)}),
                )

        def slices(panel):
            return (2 * panel, 2 * panel + 1) + (("bias",) if panel == 0 else ())

        def own_block(j):
            if not linked:
                return pltpu.make_async_copy(
                    w_hbm.at[:, :, :, :, pl.ds(j * PC, PC)], wg.at[j], lsem.at[8 + j]
                )
            return pltpu.make_async_copy(
                w_hbm.at[:, pl.ds(j * PC, PC)],
                wg.at[j, y, x, c, pl.ds(pl.multiple_of(z * R, R), R), :],
                lsem.at[8 + j],
            )

        def own_bias():
            if not linked:
                return pltpu.make_async_copy(b_hbm, brow, lsem.at[8 + panels])
            return pltpu.make_async_copy(b_hbm, bt.at[y, x, c, z], lsem.at[8 + panels])

        def gather_event(kind, panel):
            if not linked:
                if kind == "ready":
                    own_block(panel).wait()
                if kind == "ready" and panel == 0:
                    own_bias().wait()
            elif kind == "first":
                for t in slices(panel):
                    gather_first(t)
            elif kind == "second":
                for t in slices(panel):
                    gather_wait(t, 0)
                own_block(panel).wait()
                if panel == 0:
                    own_bias().wait()
                for t in slices(panel):
                    gather_send(t, 1)
            elif kind == "third":
                for t in slices(panel):
                    gather_wait(t, 1)
                for t in slices(panel):
                    gather_send(t, 2)
                for t in slices(panel):
                    core_send(t, False)
            elif kind == "pass":
                for t in slices(panel):
                    gather_wait(t, 2)
                for t in slices(panel):
                    core_send(t, True)
            elif kind == "ready":
                for t in slices(panel):
                    core_wait(t)

        load_n = lambda ref: pltpu.make_async_copy(n_hbm, ref, lsem.at[9 + panels])
        load_f = pltpu.make_async_copy(f_hbm, fg, lsem.at[10 + panels])

        def count_phase(nb, lo_s, wa_s, wb_s):
            load_n(nb).start()
            peers = [me.peer(d, o) for d in "cxyz" for o in me.offsets(d) if linked]
            for p in peers:
                pl.semaphore_signal(
                    pltpu.get_barrier_semaphore(), inc=1,
                    device_id=p, device_id_type=MESH,
                )
            for j in range(panels):
                own_block(j).start()
            own_bias().start()
            if linked:
                pl.semaphore_wait(pltpu.get_barrier_semaphore(), len(peers))
            gather_event("first", 0)
            gather_event("first", 2)
            load_f.start()
            load_n(nb).wait()

            @pl.loop(0, chunks)
            def _(q):
                r = pl.ds(pl.multiple_of(q * 128, 128), 128)
                ids = nb[r, :]
                degree = jnp.sum((ids >= 0).astype(F32), axis=1, keepdims=True)
                fac[r, :] = jnp.broadcast_to(1.0 / (degree + 1.0), (128, 128))
                ids = ids.T
                group = ids >> 7
                digit = jnp.left_shift(jnp.ones_like(ids), (group & 3) * 8)
                lo_s[:, r] = ids & 127
                wa_s[:, r] = jnp.where((group >= 0) & (group < 4), digit, 0)
                wb_s[:, r] = jnp.where(group >= 4, digit, 0)

            lane = lax.broadcasted_iota(I32, (128, 128), 0)
            twice = jnp.where(
                lane == lax.broadcasted_iota(I32, (128, 128), 1), 2.0, 0.0
            )

            @pl.loop(0, chunks)
            def _(q):
                col = pl.ds(pl.multiple_of(q * 128, 128), 128)

                def step(s, carry):
                    a, b = carry
                    rows_ = pl.ds(pl.multiple_of(s * UNROLL, UNROLL), UNROLL)
                    lo, wa, wb = lo_s[rows_, col], wa_s[rows_, col], wb_s[rows_, col]
                    for k in range(UNROLL):
                        hit = lo[k : k + 1] == lane
                        a = a + jnp.where(hit, wa[k : k + 1], 0)
                        b = b + jnp.where(hit, wb[k : k + 1], 0)
                    return a, b

                zero = jnp.zeros((128, 128), I32)
                a, b = lax.fori_loop(0, SLOTS // UNROLL, step, (zero, zero))
                cl, place = q // 8, q % 8
                to = pl.ds(pl.multiple_of(place * 128, 128), 128)
                for h in range(8):
                    count = ((a if h < 4 else b) >> (8 * (h % 4))) & 255
                    count = count.astype(F32) + jnp.where(place == h, twice, 0.0)
                    a2t[cl, pl.ds(h * 128, 128), to] = count.astype(BF16)
                for at, kind, panel in COUNT_EVENTS:
                    pl.when(q == at)(lambda k=kind, p=panel: gather_event(k, p))

        pl.run_scoped(
            count_phase,
            pltpu.VMEM((nodes, SLOTS), I32),
            *[pltpu.VMEM((SLOTS, nodes), I32)] * 3,
        )
        store_a = pltpu.make_async_copy(a2t, a_hbm, lsem.at[11 + panels])
        store_a.start()
        load_f.wait()

        @pl.loop(0, clusters * 4)
        def _(s):
            cl, i, j = s // 4, (s // 2) % 2, s % 2
            r = pl.ds(pl.multiple_of(cl * CLUSTER + i * 512, 512), 512)
            k = pl.ds(pl.multiple_of(cl * CLUSTER, CLUSTER), CLUSTER)
            col = pl.ds(pl.multiple_of(j * half_rows, half_rows), half_rows)
            links = a2t[cl, :, pl.ds(pl.multiple_of(i * 512, 512), 512)]
            total = dot(links, fg[k, col], TN)
            scale = jnp.concatenate([fac[r, :]] * (half_rows // 128), axis=1)
            mixed[r, col] = (scale * total).astype(BF16)
            for at, kind, panel in MIX_EVENTS:
                pl.when(s == at)(lambda k=kind, p=panel: gather_event(k, p))

        def linear_phase(acc_a, acc_b, go, ac):
            def where(n):
                return n // per_panel, n % per_panel

            def block(hbm, n):
                j, i = where(n)
                return hbm.at[
                    pl.ds(pl.multiple_of(i * TM, TM), TM),
                    pl.ds(pl.multiple_of(j * PC, PC), PC),
                ]

            def load_g(n, slot):
                return pltpu.make_async_copy(
                    block(g_hbm, n), go.at[slot], lsem.at[slot]
                )

            def store_act(n, slot):
                return pltpu.make_async_copy(
                    ac.at[slot], block(act_hbm, n), lsem.at[4 + slot]
                )

            def product(n):
                j, i = where(n)
                panel = wg[j].reshape(width, PC)
                return dot(mixed[pl.ds(pl.multiple_of(i * TM, TM), TM), :], panel, NN)

            def finish(acc, n, slot):
                j, i = where(n)
                r = pl.ds(pl.multiple_of(i * TM, TM), TM)
                col = pl.ds(pl.multiple_of(j * PC, PC), PC)
                v = acc[...] + brow[0:1, col]
                u = v * v
                h = 0.5 + 0.5 * jnp.tanh(v * (ALPHA + BETA * u))
                a = v * h
                d = h + (a * (1.0 - h)) * (2 * ALPHA + (6 * BETA) * u)
                g = go[slot].astype(F32) * d
                ac[slot] = a.astype(BF16)
                fg[r, col] = g.astype(BF16)
                gbacc[:, col] += jnp.sum(g.reshape(TM // 8, 8, PC), axis=0)

            gather_event("ready", 0)
            p = 128 // R
            for k in range(width // 128 if linked else 0):
                tile = jnp.zeros((8, 128), F32)
                for d in range(k * p, (k + 1) * p):
                    tile = tile + bt[d // (X * 2 * S), d // (2 * S) % X, d // S % 2, d % S]
                brow[:, pl.ds(k * 128, 128)] = tile
            gbacc[...] = jnp.zeros_like(gbacc)
            for n in range(2):
                load_g(n, n).start()
            acc_a[...] = product(0)

            def pair(t, last):
                n = 2 * t
                slot = t % 2 * 2
                load_g(n, slot).wait()
                load_g(n + 1, slot + 1).wait()
                if not last:
                    other = 2 - slot
                    load_g(n + 2, other).start()
                    load_g(n + 3, other + 1).start()

                @pl.when(jnp.asarray(t >= 2))
                def _():
                    store_act(n - 4, slot).wait()
                    store_act(n - 3, slot + 1).wait()

                acc_b[...] = product(n + 1)
                finish(acc_a, n, slot)
                if not last:
                    acc_a[...] = product(n + 2)
                finish(acc_b, n + 1, slot + 1)
                store_act(n, slot).start()
                store_act(n + 1, slot + 1).start()

            @pl.loop(0, tiles // 2 - 1)
            def _(t):
                for j in range(1, panels):

                    @pl.when(t == (per_panel // 2) * j - 1)
                    def _():
                        if j == 1:
                            gather_event("pass", 3)
                        gather_event("ready", j)

                pair(t, False)

            last = tiles // 2 - 1
            pair(last, True)
            for n in range(tiles - 4, tiles):
                store_act(n, n % 4).wait()

        pl.run_scoped(
            linear_phase,
            *[pltpu.VMEM((TM, PC), F32)] * 2,
            *[pltpu.VMEM((4, TM, PC), BF16)] * 2,
        )
        store_a.wait()

        def back_phase(pt, sp):
            half_y = Y // 2
            y_half = y // half_y

            def half_of(hh):
                if isinstance(hh, int):
                    return y_half if hh else 1 - y_half
                return jnp.where(hh == 0, 1 - y_half, y_half)

            def part(t, core, **at):
                ys, xs = at.get("y", ALL), at.get("x", ALL)
                if t == "bias":
                    zs = pl.ds(at["z"], 1) if "z" in at else ALL
                    return ptb.at[ys, xs, core, zs]
                zs = pl.ds(pl.multiple_of(at["z"] * R, R), R) if "z" in at else ALL
                return pt.at[t // 2, ys, xs, core, zs, pl.ds(t % 2 * HC, HC)]

            def scatter_path(t):
                return SCATTER[0] if t == "bias" else SCATTER[t]

            def landing(t, k):
                return stage[(len(SCATTER) if t == "bias" else t) * 3 + k]

            def scatter_send(t, k, h=None):
                path = scatter_path(t)

                def make(o):
                    at = fixed(path[:k])
                    at[path[k]] = me.shifted(path[k], o)
                    dst = landing(t, k).at[o - 1]
                    if h is not None:
                        ys = pl.ds(half_of(h) * half_y, half_y)
                        at["y"] = ys
                        dst = dst.at[ys]
                    return part(t, c, **at), dst, me.peer(path[k], o)

                for o in me.offsets(path[k]):
                    send(("scatter", t, k, o, h or 0), lambda o=o: make(o))

            def scatter_wait(t, k):
                path = scatter_path(t)
                for o in me.offsets(path[k]):
                    ref = landing(t, k).at[o - 1]
                    if t != "bias" and k == 0 and path[0] == "x":
                        for i in range(2):
                            ys = pl.ds(half_of(i) * half_y, half_y)
                            arrived(("scatter", t, k, o, i), ref.at[ys])
                    else:
                        arrived(("scatter", t, k, o, 0), ref)

            def scatter_add(t, k):
                path = scatter_path(t)
                mine = part(t, c, **fixed(path[: k + 1]))
                total = mine[...].astype(F32)
                for o in me.offsets(path[k]):
                    total = total + landing(t, k)[o - 1].astype(F32)
                if k < 2:
                    mine[...] = total.astype(mine.dtype)
                elif t == "bias":
                    gbs[...] = total.reshape(8, 128)
                else:
                    gws[:, pl.ds(t * HC, HC)] = total

            def swap(s):
                j, hh = s // 2, s % 2
                ys = pl.ds(half_of(hh) * half_y, half_y)
                i = sems["swap", 0] + s
                return pltpu.make_async_remote_copy(
                    src_ref=pt.at[j, ys, :, 1 - c], dst_ref=cr.at[j, ys],
                    send_sem=ssem.at[i], recv_sem=rsem.at[i],
                    device_id=me.peer("c", 1), device_id_type=MESH,
                )

            def core_sum(s):
                j, hh = s // 2, s % 2
                swap(s).wait_recv()
                ys = pl.ds(half_of(hh) * half_y, half_y)
                mine = pt.at[j, ys, :, c]
                mine[...] = (mine[...].astype(F32) + cr[j, ys].astype(F32)).astype(BF16)
                for t in (2 * j, 2 * j + 1):
                    if scatter_path(t)[0] == "x":
                        scatter_send(t, 0, hh)
                    elif hh == (0 if Y == 2 else 1):
                        scatter_send(t, 0)

            def scatter_event(k, j):
                ts = (2 * j, 2 * j + 1) + (("bias",) if j == 0 else ())
                for t in ts:
                    scatter_wait(t, k - 1)
                    scatter_add(t, k - 1)
                    if k < 3:
                        scatter_send(t, k)

            def store_part(s):
                j, hh = s // 2, s % 2
                ys = pl.ds(half_of(hh) * half_y, half_y)
                return pltpu.make_async_copy(
                    pt.at[j, ys],
                    gw_hbm.at[ys, :, :, :, pl.ds(pl.multiple_of(j * PC, PC), PC)],
                    lsem.at[12 + panels + s],
                )

            for d in range(n_dev if linked else 0):
                col = pl.ds(d * R // 128 * 128, 128)
                ptb[d // (X * 2 * S), d // (2 * S) % X, d // S % 2, d % S] = gbacc[:, col]
            if linked:
                send(
                    ("swap", "bias"),
                    lambda: (ptb.at[:, :, 1 - c], crb, me.peer("c", 1)),
                )

            @pl.loop(0, 2 * panels)
            def _(s):
                j, hh = s // 2, s % 2
                h = half_of(hh)
                rows_ = pl.ds(pl.multiple_of(h * half_rows, half_rows), half_rows)
                col = pl.ds(pl.multiple_of(j * PC, PC), PC)
                total = dot(mixed[:, rows_], fg[:, col], TN).astype(BF16)
                pt[j, pl.ds(h * half_y, half_y)] = total.reshape(half_y, X, 2, SR, PC)
                if not linked:
                    store_part(s).start()
                    return
                swap(s).start()

                @pl.when(s == 0)
                def _():
                    arrived(("swap", "bias"), crb)
                    mine = ptb.at[:, :, c]
                    mine[...] = mine[...] + crb[...]
                    scatter_send("bias", 0)

                for e in range(2 * panels - 1):
                    pl.when(s == e + 1)(lambda e=e: core_sum(e))
                for at, k, panel in SUM_EVENTS:
                    pl.when(s == at)(lambda k=k, p=panel: scatter_event(k, p))

            def store_sp(s):
                i, yy = s // Y, s % Y
                slot = s % 2
                return pltpu.make_async_copy(
                    sp.at[slot],
                    sp_hbm.at[
                        pl.ds(pl.multiple_of(i * TM, TM), TM),
                        pl.ds(pl.multiple_of(yy * FW, FW), FW),
                    ],
                    lsem.at[slot],
                )

            steps = nodes // TM * Y

            @pl.loop(0, steps)
            def _(s):
                i, yy = s // Y, s % Y
                r = pl.ds(pl.multiple_of(i * TM, TM), TM)
                total = None
                for j in range(panels):
                    rhs = wg[j, yy].reshape(FW, PC)
                    term = dot(fg[r, pl.ds(j * PC, PC)], rhs, NT)
                    total = term if total is None else total + term
                scale = jnp.concatenate([fac[r, :]] * (FW // 128), axis=1)

                @pl.when(s >= 2)
                def _():
                    store_sp(s - 2).wait()

                sp[lax.rem(s, 2)] = (scale * total).astype(BF16)
                store_sp(s).start()
                if not linked:
                    return
                pl.when(s == 0)(lambda: core_sum(2 * panels - 1))
                for at, k, panel in BACK_EVENTS:
                    pl.when(s == at)(lambda k=k, p=panel: scatter_event(k, p))

            for s in (steps - 2, steps - 1):
                store_sp(s).wait()
            if linked:
                scatter_event(3, panels - 1)
                out_w = pltpu.make_async_copy(gws, gw_hbm, lsem.at[2])
                out_b = pltpu.make_async_copy(gbs, gb_hbm, lsem.at[3])
            else:
                for s in range(2 * panels):
                    store_part(s).wait()
                out_b = pltpu.make_async_copy(gbacc, gb_hbm, lsem.at[3])
            out_b.start()
            if linked:
                out_w.start()
                for s in range(2 * panels):
                    swap(s).wait_send()
                for name, make in started:
                    remote(name, *make()).wait_send()
                out_w.wait()
            out_b.wait()

        pl.run_scoped(
            back_phase,
            pltpu.VMEM((panels, Y, X, 2, SR, PC), BF16),
            pltpu.VMEM((2, TM, FW), BF16),
        )

    any_spec = pl.BlockSpec(memory_space=pl.ANY)
    scratch = [
        pltpu.VMEM((nodes, width), BF16),
        pltpu.VMEM((nodes, width), BF16),
        pltpu.VMEM((panels, Y, X, 2, SR, PC), BF16),
        pltpu.VMEM((clusters, CLUSTER, CLUSTER), BF16),
        pltpu.VMEM((nodes, 128), F32),
        pltpu.VMEM((Y, X, 2, S, 8, 128), F32),
        pltpu.VMEM((8, width), F32),
        pltpu.VMEM((8, width), F32),
        pltpu.VMEM((panels, Y, X, SR, PC), BF16),
        pltpu.VMEM((Y, X, S, 8, 128), F32),
        pltpu.VMEM((Y, X, 2, S, 8, 128), F32),
        pltpu.VMEM((R, width), F32),
        pltpu.VMEM((8, 128), F32),
        *stage_shapes(),
        pltpu.SemaphoreType.DMA((n_sems,)),
        pltpu.SemaphoreType.DMA((n_sems,)),
        pltpu.SemaphoreType.DMA((12 + 3 * panels,)),
    ]
    if not linked:
        for k in (5, 8, 9, 10, 11, 12, *range(13, 13 + n_stage)):
            scratch[k] = pltpu.VMEM((8, 128), F32)
        scratch[-3] = scratch[-2] = pltpu.SemaphoreType.DMA((1,))
    return pl.pallas_call(
        kernel,
        out_shape=(
            jax.ShapeDtypeStruct((nodes, width), BF16),
            jax.ShapeDtypeStruct((nodes, width), BF16),
            jax.ShapeDtypeStruct((clusters, CLUSTER, CLUSTER), BF16),
            jax.ShapeDtypeStruct((R, width), F32)
            if linked
            else jax.ShapeDtypeStruct((Y, X, 2, SR, width), BF16),
            jax.ShapeDtypeStruct((8, 128 if linked else width), F32),
        ),
        in_specs=[any_spec] * 5,
        out_specs=(any_spec,) * 5,
        scratch_shapes=scratch,
        compiler_params=pltpu.CompilerParams(
            collective_id=0 if linked else None,
            has_side_effects=True,
            vmem_limit_bytes=60 * 2**20,
        ),
        name="layer",
    )


def last_kernel(a_ref, sp_ref, act_in, out_ref, act_out, held, in_sem, out_sem):
    step = pl.program_id(0) * pl.num_programs(1) + pl.program_id(1)
    count, rows = held.shape[0], held.shape[1]

    def inward(k):
        part = act_in.at[pl.ds(k * rows, rows)]
        return pltpu.make_async_copy(part, held.at[k], in_sem.at[k])

    def outward(k):
        part = act_out.at[pl.ds(k * rows, rows)]
        return pltpu.make_async_copy(held.at[k], part, out_sem.at[k])

    @pl.when(step == 0)
    def _():
        for k in range(count):
            inward(k).start()

    out_ref[...] = dot(a_ref[0], sp_ref[...], NN)
    for k in range(count):

        @pl.when(step == k)
        def _():
            inward(k).wait()
            outward(k).start()

    @pl.when(step == count - 1)
    def _():
        for k in range(count):
            outward(k).wait()


def last(links, spread, act):
    nodes, width = spread.shape
    tile = 512
    steps = nodes // CLUSTER * (width // tile)
    return pl.pallas_call(
        last_kernel,
        out_shape=(
            jax.ShapeDtypeStruct((nodes, width), F32),
            jax.ShapeDtypeStruct((nodes, width), BF16),
        ),
        grid=(nodes // CLUSTER, width // tile),
        in_specs=[
            pl.BlockSpec((1, CLUSTER, CLUSTER), lambda i, j: (i, 0, 0)),
            pl.BlockSpec((CLUSTER, tile), lambda i, j: (i, j)),
            pl.BlockSpec(memory_space=pl.ANY),
        ],
        out_specs=(
            pl.BlockSpec((CLUSTER, tile), lambda i, j: (i, j)),
            pl.BlockSpec(memory_space=pl.ANY),
        ),
        scratch_shapes=[
            pltpu.VMEM((steps, nodes // steps, width), BF16),
            pltpu.SemaphoreType.DMA((steps,)),
            pltpu.SemaphoreType.DMA((steps,)),
        ],
        compiler_params=pltpu.CompilerParams(vmem_limit_bytes=60 * 2**20),
        name="features",
    )(links, spread, act)


def solution(mesh):
    dp_size, shard_size = mesh.shape["dp"], mesh.shape["shard"]

    def on_device(features, neighbors, weight, bias_terms, grad_out):
        nodes, width = features.shape
        rows = weight.shape[0]
        layer = make_kernel(dp_size, shard_size, rows, width, nodes)
        if not linkable(rows):
            both = ("dp", "shard")
            full = lax.all_gather(weight, both, axis=0, tiled=True)
            bias = lax.all_gather(bias_terms, both, axis=0, tiled=True).astype(F32)
            act, spread, links, parts, bias_sums = layer(
                features,
                neighbors,
                full.reshape(dp_size // 4, 2, 2, shard_size * rows, width),
                jnp.broadcast_to(bias, (8, width)),
                grad_out,
            )
            grad_features, output = last(links, spread, act)
            parts = parts.reshape(width, width).astype(F32)
            bias_sums = jnp.sum(bias_sums, axis=0)
            return (
                output,
                grad_features,
                lax.psum_scatter(parts, both, scatter_dimension=0, tiled=True),
                lax.psum_scatter(bias_sums, both, scatter_dimension=0, tiled=True),
            )
        device = lax.axis_index("dp") * shard_size + lax.axis_index("shard")
        lane = lax.rem(device * rows, 128)
        bias_tile = lax.dynamic_update_slice(
            jnp.zeros((8, 128), F32),
            jnp.broadcast_to(bias_terms.astype(F32), (8, rows)),
            (0, lane),
        )
        act, spread, links, grad_weight, bias_sums = layer(
            features, neighbors, weight, bias_tile, grad_out
        )
        grad_features, output = last(links, spread, act)
        grad_bias = lax.dynamic_slice(jnp.sum(bias_sums, axis=0), (lane,), (rows,))
        return output, grad_features, grad_weight, grad_bias

    split = P(("dp", "shard"), None)
    flat = P(("dp", "shard"))
    return jax.shard_map(
        on_device,
        mesh=mesh,
        in_specs=(split, split, split, flat, split),
        out_specs=(split, split, split, flat),
        check_vma=False,
    )
```

time: 1930 us -> 185 us (0.10)
  other arithmetic: 1440 us -> 0.7 us
  waiting for transfers between devices: 274 us -> 0 us
  Pallas kernels: 0 us -> 180 us
  matrix products: 109 us -> 0 us
  blocking collectives: 85 us -> 0 us
    unnamed x4 -> x0, other arithmetic: 1410 us -> none
    reduce_scatter x1 -> x0, waiting for transfers between devices: 273 us -> none  [on_device(): lax.psum_scatter(local_weight, ('dp', 'shard'), scatter_dimension=0, tile...]
    pallas_call x0 -> x2, Pallas kernels: none -> 180 us  [the longest x1 158 us: on_device(): layer(features, neighbors, weight, bias_tile, grad_out)]
    dot_general x5 -> x0, matrix products: 109 us -> none  [the longest x1 38.1 us: on_device(): jnp.dot(mixed_rows, full_weight, preferred_element_type=jnp.float32)]
    unnamed x2 -> x0, blocking collectives: 85 us -> none
  transfers between devices with their start and end apart: 2 -> 0, of which waited for: 1 -> 0; matrix products, arithmetic and copies ran while one was open for 77% -> 0% of each run, Pallas kernels for 0% -> 0%
where the time goes in v1:
time: 185 us
  Pallas kernels  180 us (97%)
  local copies, waits for them, and re-layouts  2.71 us (1%)
    pallas_call x1, Pallas kernels, on_device(): layer(features, neighbors, weight, bias_tile, grad_out)  158 us
    pallas_call x1, Pallas kernels, last(): pl.pallas_call(last_kernel, out_shape=(jax.ShapeDtypeStruct((nodes, width...  22.4 us

profile of v1, /device:TPU:0, one launch (start us, length us, event | category | flops | bytes accessed | tf_op | source)
XLA Modules:
  0.0 184.5 jit_solution(4695898914699972563)
XLA Ops:
  0.6 0.7 broadcast_in_dim.7
  1.3 0.1 dynamic_update_slice.3.b_hbm
  1.4 0.0 copy-start.1
  1.4 0.6 copy-done.1
  2.0 158.1 %layer.1 = (bf16[2048,2048]{1,0:T(8,128)(2,1)}, bf16[2048,2048]{1,0:T(8,128)(2,1)}, bf16[2,1024,1024]{2,1,0:T(8,128)(2,1)}, f32[64,2048]{1,0:T(8,128)}, f32[8,128]{1,0:T(8,128)}) custom-call(bf16[2048,2048]{1,0:T(8,128)(2,1)} %f_hbm.1, s32[2048,128]{1,0:T(8,128)} %n_hbm.1, bf16[64,2048]{1,0:T(8,128)(2,1)} %w_hbm.1, f32[8,128]{1,0:T(8,128)} %copy-done.1, ...), custom_call_target="tpu_custom_call" | custom-call | tf_op jit(solution)/shard_map/layer/pallas_call | solution.py:819
  160.1 0.7 reduce_sum.9
  160.8 0.6 dynamic_slice.3
  161.3 0.0 copy-start
  161.3 22.4 %features.1 = (f32[2048,2048]{1,0:T(8,128)}, bf16[2048,2048]{1,0:T(8,128)(2,1)}) custom-call(bf16[2,1024,1024]{2,1,0:T(8,128)(2,1)} %get-tuple-element.11.a_ref, bf16[2048,2048]{1,0:T(8,128)(2,1)} %get-tuple-element.12.sp_ref, bf16[2048,2048]{1,0:T(8,128)(2,1)} %get-tuple-element.13.act_in), custom_call_target="tpu_custom_call" | custom-call | tf_op jit(solution)/shard_map/features/pallas_call | solution.py:759
  183.7 0.0 copy-done
  183.7 0.8 copy.11
  (1 shorter events, 0.0 us)
Async XLA Ops:
  1.4 0.6 copy-start.1
  161.3 22.4 %copy-start = (f32[64,2048]{1,0:T(8,128)S(1)}, f32[64,2048]{1,0:T(8,128)}, u32[]{:S(2)}) copy-start(f32[64,2048]{1,0:T(8,128)} %get-tuple-element.24) | copy-start | bytes 1572868
